TPU v7x, 32 devices: a whole 2x2x4 slice. The times are simulated.
32 devices in a mesh: ctx: 4 (over y, x), head: 8 (over z, core).
Axes of the slice: x: 2, y: 2, z: 4, core: 2. Of those that a mesh axis runs over, the one named last changes fastest.
Arguments:
- queries: bfloat16 [2, 1024, 8192], P(None, 'ctx', 'head'), may hold values from -4.5 to 4.5
- key_rows: bfloat16 [2, 1024, 512], P(None, 'ctx'), may hold values from -4.5 to 4.5
- value_rows: bfloat16 [2, 1024, 512], P(None, 'ctx'), may hold values from -6 to 6
- out_weight: bfloat16 [8192, 8192], P('head'), may hold values from -0.0625 to 0.0625
- span_owner: int32 [2, 4], replicated, may hold values from 0 to 3, each once within a row
- vertical_blocks: int32 [64, 4], replicated, may hold values from 0 to 15, as said below
- slash_offsets: int32 [64, 4], replicated, may hold values from 1 to 15, as said below
Outputs:
- projected: bfloat16 [2, 1024, 8192], P(None, ('ctx', 'head'))
Inputs may be any that keep to these rules, and one draw needn't show every extreme that they name: `vertical_blocks`: the 4 entries of a head are distinct block numbers. `slash_offsets`: the 4 entries of a head are distinct.
All inputs are finite; a program needn't handle non-finite values.
Results may differ from a plain program's by a relative error of at most 0.017.
Values may be sent and summed in bfloat16 or wider, within the bound.
A program may use at most 64 MiB of HBM per device.

v0:
```python
import math

import jax
import jax.numpy as jnp
from jax import lax
from jax.sharding import PartitionSpec as P

QH = 64
KVH = 4
HD = 128
BLK = 128
STEPS = 2


def tile_blocks(block_ids, vertical, slanted, owner_flat, span_blocks, span_count):
    column = block_ids[:, None]
    vert_rows = jnp.broadcast_to(vertical[None, :], (block_ids.shape[0], vertical.shape[0]))
    slash_rows = column - slanted[None, :]
    vert_valid = vert_rows < column
    repeated = jnp.any(slash_rows[:, :, None] == vertical[None, None, :], axis=2)
    slash_valid = (slash_rows >= 0) & jnp.logical_not(repeated)
    chosen = jnp.concatenate([column, vert_rows, slash_rows], axis=1)
    allowed = jnp.concatenate([jnp.ones_like(column, dtype=bool), vert_valid, slash_valid], axis=1)
    chosen = jnp.where(allowed, chosen, column)
    span_index = chosen // span_blocks
    slot_ids = jnp.arange(owner_flat.shape[0], dtype=jnp.int32)
    holder = jnp.sum(
        jnp.where(span_index[:, :, None] == slot_ids[None, None, :], owner_flat[None, None, :], 0),
        axis=2,
    )
    step_index = span_index // span_count
    stored = (step_index * span_count + holder) * span_blocks + chosen % span_blocks
    return (stored, allowed)


def block_mask(allowed, block_rows):
    positions = jnp.arange(block_rows, dtype=jnp.int32)
    causal = positions[None, :] <= positions[:, None]
    tile_count = allowed.shape[1]
    first_tile = jnp.arange(tile_count, dtype=jnp.int32) == 0
    inside = causal[None, :, None, :] | jnp.logical_not(first_tile)[None, None, :, None]
    visible = allowed[:, None, :, None] & inside
    return visible.reshape(allowed.shape[0], block_rows, tile_count * block_rows)


def attend_tiles(query_tile_set, key_store, value_store, stored, allowed):
    block_count = stored.shape[0]
    tile_count = stored.shape[1]
    block_rows = query_tile_set.shape[1]
    head_features = query_tile_set.shape[2]
    key_tile_set = jnp.take(key_store, stored.reshape(-1), axis=0).reshape(
        block_count, tile_count * block_rows, head_features
    )
    value_tile_set = jnp.take(value_store, stored.reshape(-1), axis=0).reshape(
        block_count, tile_count * block_rows, head_features
    )
    logit_scores = jnp.einsum(
        "zcs,zvs->zcv", query_tile_set, key_tile_set, preferred_element_type=jnp.float32
    ) * (1.0 / math.sqrt(head_features))
    logit_scores = jnp.where(block_mask(allowed, block_rows), logit_scores, -jnp.inf)
    largest = jnp.max(logit_scores, axis=2, keepdims=True)
    weights = jnp.exp(logit_scores - largest)
    totals = jnp.sum(weights, axis=2, keepdims=True)
    mixed_output = jnp.einsum(
        "ynj,yjw->ynw",
        weights.astype(jnp.bfloat16),
        value_tile_set,
        preferred_element_type=jnp.float32,
    )
    return (mixed_output / totals).astype(jnp.bfloat16)


def local(queries, key_rows, value_rows, out_weight, span_owner, vertical_blocks, slash_offsets):
    local_heads = queries.shape[2] // HD
    span_rows = queries.shape[1]
    span_blocks = span_rows // BLK
    span_count = lax.axis_size("ctx")
    head_groups = lax.axis_size("head")
    rows_share = span_rows // head_groups
    first_head = lax.axis_index("head") * local_heads
    kv_head = first_head // (QH // KVH)
    vertical = lax.dynamic_slice_in_dim(vertical_blocks, first_head, local_heads, 0)
    slanted = lax.dynamic_slice_in_dim(slash_offsets, first_head, local_heads, 0)
    own_keys = lax.dynamic_slice_in_dim(key_rows, kv_head * HD, HD, 2)
    own_values = lax.dynamic_slice_in_dim(value_rows, kv_head * HD, HD, 2)
    paired = jnp.stack([own_keys, own_values], axis=1)
    owner_flat = span_owner.reshape(-1)
    device = lax.axis_index("ctx")
    device_ids = jnp.arange(span_count, dtype=jnp.int32)
    places = jnp.sum(device_ids[None, :] * (span_owner == device).astype(jnp.int32), axis=1)
    tiler = jax.vmap(tile_blocks, in_axes=(None, 0, 0, None, None, None))
    gathered = lax.all_gather(paired, "ctx", axis=2, tiled=True)
    outputs = []
    for current in range(STEPS):
        kv_store = gathered[: current + 1]
        key_store = kv_store[:, 0].reshape(-1, BLK, HD)
        value_store = kv_store[:, 1].reshape(-1, BLK, HD)
        block_ids = (current * span_count + places[current]) * span_blocks + jnp.arange(
            span_blocks, dtype=jnp.int32
        )
        stored, allowed = tiler(block_ids, vertical, slanted, owner_flat, span_blocks, span_count)
        stored = stored.reshape(local_heads * span_blocks, -1)
        allowed = allowed.reshape(local_heads * span_blocks, -1)
        query_tile_set = (
            queries[current]
            .reshape(span_blocks, BLK, local_heads, HD)
            .transpose(2, 0, 1, 3)
            .reshape(local_heads * span_blocks, BLK, HD)
        )
        result_tiles = attend_tiles(query_tile_set, key_store, value_store, stored, allowed)
        attended = (
            result_tiles.reshape(local_heads, span_blocks, BLK, HD)
            .transpose(1, 2, 0, 3)
            .reshape(span_rows, local_heads * HD)
        )
        outputs.append(attended)
    arranged = (
        jnp.stack(outputs)
        .reshape(STEPS, head_groups, rows_share, -1)
        .transpose(1, 0, 2, 3)
        .reshape(STEPS * span_rows, -1)
    )
    summed = lax.psum_scatter(
        jnp.dot(arranged, out_weight, preferred_element_type=jnp.float32).astype(jnp.bfloat16),
        "head",
        scatter_dimension=0,
        tiled=True,
    ).astype(jnp.float32)
    return summed.reshape(STEPS, rows_share, -1).astype(jnp.bfloat16)


def solution(mesh):
    in_specs = (
        P(None, "ctx", "head"),
        P(None, "ctx", None),
        P(None, "ctx", None),
        P("head", None),
        P(),
        P(),
        P(),
    )
    out_specs = P(None, ("ctx", "head"), None)
    return jax.shard_map(local, mesh=mesh, in_specs=in_specs, out_specs=out_specs, check_vma=False)
```

profile of v0, /device:TPU:17, one launch (start us, length us, event | category | flops | bytes accessed | tf_op | source)
XLA Modules:
  0.0 216.1 jit_solution(5318682791842009869)
XLA Ops:
  6.5 1.0 dynamic-slice_bitcast_fusion
  7.5 0.7 pad_maximum_fusion
  8.3 0.8 broadcast_in_dim_reshape.2
  9.1 0.8 fusion.24
  9.9 0.6 fusion.29
  11.8 0.8 constant_dynamic-slice_fusion
  13.1 0.1 copy.54
  13.2 0.1 copy.55
  14.2 0.1 select_reduce_fusion.1
  14.8 0.1 and.141
  15.0 1.3 slice_bitcast_fusion.1
  16.8 0.2 bitcast_or_fusion
  17.1 19.8 %all-gather.2.cloned.1.call-done = bf16[2,2,1024,128]{3,2,0,1:T(8,128)(2,1)} async-done(((bf16[2,2,256,128]{3,2,0,1:T(8,128)(2,1)}), bf16[2,2,1024,128]{3,2,0,1:T(8,128)(2,1)}) %all-gather.2.cloned.1.call-update) | async-done | bytes 1048592 | tf_op jit(solution)/shard_map/all_gather | solution.py:92
  36.9 1.3 fusion.28
  38.2 7.6 %gather_fusion.3 = bf16[144,128,128]{2,1,0:T(8,128)(2,1)} fusion(bf16[16,128,128]{2,1,0:T(8,128)(2,1)S(1)} %bitcast.81, s32[1024]{0:T(1024)S(1)} %pad_clamp_fusion), kind=kCustom, calls=%fused_computation.3.clone | custom fusion | bytes 9437760 | tf_op jit(solution)/shard_map/jit(_take)/gather | solution.py:54
  45.8 7.5 %gather_fusion.2 = bf16[144,128,128]{2,1,0:T(8,128)(2,1)} fusion(bf16[16,128,128]{2,1,0:T(8,128)(2,1)S(1)} %bitcast.80, s32[1024]{0:T(1024)S(1)} %pad_clamp_fusion), kind=kCustom, calls=%fused_computation.1.clone | custom fusion | bytes 9437760 | tf_op jit(solution)/shard_map/jit(_take)/gather | solution.py:51
  53.3 4.4 %broadcast_select_fusion.1 = (bf16[144,128,128]{2,1,0:T(8,128)(2,1)S(1)}, bf16[144,128,128]{2,1,0:T(8,128)(2,1)S(1)}) fusion(bf16[144,128,128]{2,1,0:T(8,128)(2,1)} %gather_fusion.2, pred[144]{0:T(512)(128)(4,1)S(1)} %get-tuple-element.13, bf16[144,128,128]{2,1,0:T(8,128)(2,1)} %gather_fusion.3), kind=kLoop, calls=%fused_computation.18 | loop fusion | flops 4718592 | bytes 18874512 | tf_op jit(solution)/shard_map/jit(_take)/select_n | solution.py:51
  57.7 9.0 %fusion.30 = (f32[16,128]{1,0:T(8,128)S(1)}, f32[16,128,1152]{1,2,0:T(8,128)S(1)}) fusion(bf16[16,1152,128]{2,1,0:T(8,128)(2,1)S(1)} %bitcast.85, bf16[16,128,128]{2,1,0:T(8,128)(2,1)S(1)} %bitcast.94, pred[128,1152]{0,1:T(8,128)(4,1)S(1)} %bitcast_or_fusion, pred[16,1152]{1,0:T(8,128)(4,1)S(1)} %bitcast.100), kind=kOutput, calls=%fused_computation.112 | convolution fusion | flops 613414912 | bytes 14854144 | tf_op jit(solution)/shard_map/zcs,zvs->zcv/dot_general | solution.py:57
  66.7 1.3 fusion.2
  68.0 2.5 %divide_convert_fusion = bf16[16,128,128]{2,1,0:T(8,128)(2,1)S(1)} fusion(bf16[16,1152,128]{2,1,0:T(8,128)(2,1)S(1)} %bitcast.83, f32[16,128,1152]{1,2,0:T(8,128)S(1)} %get-tuple-element.50, f32[16,128]{1,0:T(8,128)S(1)} %get-tuple-element.49, f32[16,128]{1,0:T(8,128)S(1)} %fusion.2), kind=kOutput, calls=%fused_computation.22 | convolution fusion | flops 609222656 | bytes 14696448 | tf_op jit(solution)/shard_map/ynj,yjw->ynw/dot_general | solution.py:64
  70.5 0.3 copy.68
  70.8 0.2 stack.20
  71.1 7.6 %gather_fusion.1 = bf16[144,128,128]{2,1,0:T(8,128)(2,1)} fusion(bf16[8,128,128]{2,1,0:T(8,128)(2,1)S(1)} %bitcast.79, s32[1024]{0:T(1024)S(1)} %pad_clamp_fusion.1), kind=kCustom, calls=%fused_computation.2.clone | custom fusion | bytes 9437760 | tf_op jit(solution)/shard_map/jit(_take)/gather | solution.py:54
  78.7 7.7 %gather_fusion = bf16[144,128,128]{2,1,0:T(8,128)(2,1)} fusion(bf16[8,128,128]{2,1,0:T(8,128)(2,1)S(1)} %bitcast.78, s32[1024]{0:T(1024)S(1)} %pad_clamp_fusion.1), kind=kCustom, calls=%fused_computation.clone | custom fusion | bytes 9437760 | tf_op jit(solution)/shard_map/jit(_take)/gather | solution.py:51
  86.4 4.4 %broadcast_select_fusion.3 = (bf16[144,128,128]{2,1,0:T(8,128)(2,1)S(1)}, bf16[144,128,128]{2,1,0:T(8,128)(2,1)S(1)}) fusion(bf16[144,128,128]{2,1,0:T(8,128)(2,1)} %gather_fusion, pred[144]{0:T(512)(128)(4,1)S(1)} %get-tuple-element.53, bf16[144,128,128]{2,1,0:T(8,128)(2,1)} %gather_fusion.1), kind=kLoop, calls=%fused_computation.20 | loop fusion | flops 4718592 | bytes 18874512 | tf_op jit(solution)/shard_map/jit(_take)/select_n | solution.py:51
  90.8 9.0 %fusion.31 = (f32[16,128]{1,0:T(8,128)S(1)}, f32[16,128,1152]{1,2,0:T(8,128)S(1)}) fusion(bf16[16,1152,128]{2,1,0:T(8,128)(2,1)S(1)} %bitcast.84, bf16[16,128,128]{2,1,0:T(8,128)(2,1)S(1)} %bitcast.93, pred[128,1152]{0,1:T(8,128)(4,1)S(1)} %bitcast_or_fusion, pred[16,1152]{1,0:T(8,128)(4,1)S(1)} %bitcast.99), kind=kOutput, calls=%fused_computation.113 | convolution fusion | flops 613414912 | bytes 14854144 | tf_op jit(solution)/shard_map/zcs,zvs->zcv/dot_general | solution.py:57
  99.8 1.2 fusion
  101.0 2.5 %divide_convert_fusion.1 = bf16[16,128,128]{2,1,0:T(8,128)(2,1)S(1)} fusion(bf16[16,1152,128]{2,1,0:T(8,128)(2,1)S(1)} %bitcast.82, f32[16,128,1152]{1,2,0:T(8,128)S(1)} %get-tuple-element.52, f32[16,128]{1,0:T(8,128)S(1)} %get-tuple-element.51, f32[16,128]{1,0:T(8,128)S(1)} %fusion), kind=kOutput, calls=%fused_computation.23 | convolution fusion | flops 609222656 | bytes 14696448 | tf_op jit(solution)/shard_map/ynj,yjw->ynw/dot_general | solution.py:64
  103.6 0.3 copy.69
  103.9 0.2 stack.19
  104.3 16.8 %convolution_convert_fusion = bf16[512,8192]{1,0:T(8,128)(2,1)} fusion(bf16[512,1024]{1,0:T(8,128)(2,1)S(1)} %bitcast.92, bf16[1024,8192]{1,0:T(8,128)(2,1)} %param.14), kind=kOutput, calls=%fused_computation.4 | convolution fusion | flops 8594128896 | bytes 26214400 | tf_op jit(solution)/shard_map/dot_general | solution.py:124
  121.2 88.1 %reduce-scatter.2.cloned.1.call-done = bf16[64,8192]{1,0:T(8,128)(2,1)} async-done(((bf16[512,8192]{1,0:T(8,128)(2,1)}), bf16[64,8192]{1,0:T(8,128)(2,1)}) %reduce-scatter.2.cloned.1.call-update) | async-done | bytes 1048592 | tf_op jit(solution)/shard_map/reduce_scatter | solution.py:123
  (58 shorter events, 2.8 us)
Async XLA Ops:
  6.5 5.2 %copy-start = (s32[64,4]{0,1:T(4,128)S(1)}, s32[64,4]{0,1:T(4,128)}, u32[]{:S(2)}) copy-start(s32[64,4]{0,1:T(4,128)} %param.16) | copy-start | bytes 3076
  6.5 30.4 %all-gather.2.cloned.1.call-start = ((), (), s32[]{:S(2)}) async-start(), calls=%async_computation.1 | async-start | bytes 1310720 | tf_op jit(solution)/shard_map/all_gather | solution.py:92
  8.3 200.9 %reduce-scatter.2.cloned.1.call-start = ((), (), s32[]{:S(2)}) async-start(), calls=%async_computation.2 | async-start | bytes 9437184 | tf_op jit(solution)/shard_map/reduce_scatter | solution.py:123
  68.0 3.1 %copy-start.2 = (bf16[2,2,1024,128]{3,2,0,1:T(8,128)(2,1)S(1)}, bf16[2,2,1024,128]{3,2,0,1:T(8,128)(2,1)}, u32[]{:S(2)}) copy-start(bf16[2,2,1024,128]{3,2,0,1:T(8,128)(2,1)} %all-gather.2.cloned.1.call-done) | copy-start | bytes 3145732
  104.3 104.9 %copy-start.1 = (s32[64,4]{0,1:T(4,128)S(1)}, s32[64,4]{0,1:T(4,128)}, u32[]{:S(2)}) copy-start(s32[64,4]{0,1:T(4,128)} %param.16) | copy-start | bytes 3076
Sparse Core Ops, SparseCore 0:
  9.2 27.6 all-gather.1
  121.3 87.8 reduce-scatter.1
where the time goes:
time: 220 us; the launch traced here: 216 us
  waiting for transfers between devices  108 us (49%)
  matrix products  39.8 us (18%)
  local copies, waits for them, and re-layouts  39.5 us (18%)
  between operations  15 us (7%)
  other arithmetic  13.9 us (6%)
    reduce_scatter x1, waiting for transfers between devices, local(): lax.psum_scatter(jnp.dot(arranged, out_weight, preferred_element_type=jnp...  88.1 us
    all_gather x1, waiting for transfers between devices, local(): gathered = lax.all_gather(paired, 'ctx', axis=2, tiled=True)  19.8 us
    dot_general x2, matrix products, attend_tiles(): jnp.einsum('zcs,zvs->zcv', query_tile_set, key_tile_set, preferred_elemen...  17.9 us
    dot_general x1, matrix products, local(): jnp.dot(arranged, out_weight, preferred_element_type=jnp.float32)  16.8 us
    gather x2, local copies, waits for them, and re-layouts, attend_tiles(): jnp.take(key_store, stored.reshape(-1), axis=0)  15.2 us
    gather x2, local copies, waits for them, and re-layouts, attend_tiles(): jnp.take(value_store, stored.reshape(-1), axis=0)  15.1 us
    select_n x2, other arithmetic, attend_tiles(): jnp.take(key_store, stored.reshape(-1), axis=0)  8.79 us
    dot_general x2, matrix products, attend_tiles(): jnp.einsum('ynj,yjw->ynw', weights.astype(jnp.bfloat16), value_tile_set,...  5.04 us
  transfers between devices with their start and end apart: 2, of which 2 were waited for; matrix products, arithmetic and copies ran while one was open for 3% of the time, Pallas kernels for 0%

commit v1 on v0

v1 whole, which is shorter than its diff:
```python
import functools
import math

import jax
import jax.numpy as jnp
from jax import lax
from jax.experimental import pallas as pl
from jax.experimental.pallas import tpu as pltpu
from jax.sharding import PartitionSpec as P

QH = 64
KVH = 4
HD = 128
BLK = 128
STEPS = 2
NW = 1024
MESH = pl.DeviceIdType.MESH


def kernel(
    C, H, LH, RS, NV, NS,
    owner, vert, slant, q_hbm, k_hbm, v_hbm, w_hbm, out_hbm,
    q_ref, k0, k1, v0, v1, w_ref, att, part, crecv, urecv, drecv, obuf, tab_idx, tab_bias,
    load_sem, w_sem, own_sem, kv_send, kv_recv, fw_send, fw_recv,
    x_send, x_recv, z_send, u_recv, d_recv, o_sem, early_sem,
):
    Z = H // 2
    NC = w_ref.shape[0]
    SB = q_ref.shape[1] // BLK
    QR = 2 * RS
    NT = 1 + NV + NS
    c = lax.axis_index("ctx")
    h = lax.axis_index("head")
    z = h // 2
    j = h % 2
    sib = z * 2 + 1 - j
    kbufs, vbufs = (k0, k1), (v0, v1)

    kv_head = (h * LH) // (QH // KVH)
    cols = pl.ds(pl.multiple_of(kv_head * HD, HD), HD)
    own_rows = pl.ds(pl.multiple_of(j * BLK, BLK), BLK)

    own_copies = []
    for s in range(STEPS):
        for t, (src, bufs) in enumerate(((k_hbm, kbufs), (v_hbm, vbufs))):
            for b in range(SB):
                cp = pltpu.make_async_copy(
                    src.at[s, pl.ds(b * BLK, BLK), cols], bufs[s].at[s * C * SB + SB * c + b], own_sem.at[s, t, b]
                )
                cp.start()
                own_copies.append((s, cp))
    q_copy = pltpu.make_async_copy(q_hbm, q_ref, load_sem)
    q_copy.start()

    def w_copy(n):
        return pltpu.make_async_copy(
            w_hbm.at[:, pl.ds(pl.multiple_of(n * NW, NW), NW)], w_ref.at[n], w_sem.at[n]
        )

    barrier = pltpu.get_barrier_semaphore()
    pl.semaphore_signal(barrier, inc=1, device_id={"head": sib}, device_id_type=MESH)

    @pl.when(z > 0)
    def _():
        pl.semaphore_signal(barrier, inc=1, device_id={"head": h - 2}, device_id_type=MESH)

    @pl.when(z < Z - 1)
    def _():
        pl.semaphore_signal(barrier, inc=1, device_id={"head": h + 2}, device_id_type=MESH)

    for p in range(1, C):
        pl.semaphore_signal(barrier, inc=1, device_id={"ctx": lax.rem(c + p, C)}, device_id_type=MESH)
    pl.semaphore_wait(barrier, C + (z > 0).astype(jnp.int32) + (z < Z - 1).astype(jnp.int32))

    def kv_copy(s, t, p):
        src = (k_hbm, v_hbm)[t]
        buf = (kbufs, vbufs)[t][s]
        return pltpu.make_async_remote_copy(
            src_ref=src.at[s, own_rows, cols],
            dst_ref=buf.at[s * C * SB + SB * c + j],
            send_sem=kv_send.at[s, t, p],
            recv_sem=kv_recv.at[s, t, c],
            device_id={"ctx": lax.rem(c + p, C)},
            device_id_type=MESH,
        )

    def kv_arrival(s, t, origin, block, sem):
        buf = (kbufs, vbufs)[t][s]
        dst = buf.at[s * C * SB + SB * origin + block]
        return pltpu.make_async_copy(dst, dst, sem.at[s, t, origin])

    def fw_copy(s, t, p):
        origin = lax.rem(c + C - p, C)
        buf = (kbufs, vbufs)[t][s]
        return pltpu.make_async_remote_copy(
            src_ref=buf.at[s * C * SB + SB * origin + j],
            dst_ref=buf.at[s * C * SB + SB * origin + j],
            send_sem=fw_send.at[s, t, p],
            recv_sem=fw_recv.at[s, t, origin],
            device_id={"head": sib},
            device_id_type=MESH,
        )

    for s in range(STEPS):
        for p in range(1, C):
            for t in range(2):
                kv_copy(s, t, p).start()
    for n in range(NC):
        w_copy(n).start()

    for s in range(STEPS):
        place = jnp.int32(0)
        for p in range(C):
            place = jnp.where(owner[s, p] == c, p, place)

        def fill(i, carry, s=s, place=place):
            b = i // LH
            lh = i % LH
            head = h * LH + lh
            block = (s * C + place) * SB + b

            def put(tile, chosen, allowed):
                chosen = jnp.where(allowed, chosen, block)
                span = chosen // SB
                step = span // C
                holder = owner[step, span - step * C]
                tab_idx[s, i, tile] = (step * C + holder) * SB + chosen - span * SB
                tab_bias[s, i, tile] = jnp.where(allowed, 0.0, -1e30).astype(jnp.float32)

            vs = [vert[head, a] for a in range(NV)]
            put(0, block, block == block)
            for a in range(NV):
                put(1 + a, vs[a], vs[a] < block)
            for a in range(NS):
                row = block - slant[head, a]
                ok = row >= 0
                for x in vs:
                    ok = jnp.logical_and(ok, row != x)
                put(1 + NV + a, row, ok)
            return carry

        lax.fori_loop(0, SB * LH, fill, 0)

    scale = math.log2(math.e) / math.sqrt(HD)

    def attend(d, s):
        r0 = pl.multiple_of(d * QR, QR)
        b = r0 // BLK
        within = r0 - b * BLK
        row_ids = lax.broadcasted_iota(jnp.int32, (QR, BLK), 0) + within
        col_ids = lax.broadcasted_iota(jnp.int32, (QR, BLK), 1)
        causal = col_ids <= row_ids

        def one(lh):
            hc = pl.ds(pl.multiple_of(lh * HD, HD), HD)
            i = b * LH + lh
            qt = q_ref[s, pl.ds(r0, QR), hc]
            ids = [tab_idx[s, i, t] for t in range(NT)]

            def tile(bufs, t):
                return bufs[s][ids[t]]

            kt = jnp.concatenate([tile(kbufs, t) for t in range(NT)], axis=0)
            sc = lax.dot_general(qt, kt, (((1,), (1,)), ((), ())), preferred_element_type=jnp.float32)
            pieces = []
            for t in range(NT):
                x = sc[:, t * BLK:(t + 1) * BLK] * scale
                if t == 0:
                    x = jnp.where(causal, x, -1e30)
                else:
                    x = x + tab_bias[s, i, t]
                pieces.append(x)
            top = pieces[0]
            for x in pieces[1:]:
                top = jnp.maximum(top, x)
            top = jnp.max(top, axis=1, keepdims=True)
            ws = [jnp.exp2(x - top) for x in pieces]
            tot = ws[0]
            for x in ws[1:]:
                tot = tot + x
            tot = jnp.sum(tot, axis=1, keepdims=True)
            wt = jnp.concatenate([x.astype(jnp.bfloat16) for x in ws], axis=1)
            vt = jnp.concatenate([tile(vbufs, t) for t in range(NT)], axis=0)
            mixed = jnp.dot(wt, vt, preferred_element_type=jnp.float32) / tot
            mixed = mixed.astype(jnp.bfloat16)
            att[pl.ds(s * RS, RS), hc] = mixed[:RS]
            att[pl.ds((STEPS + s) * RS, RS), hc] = mixed[RS:]

        def body(i, carry):
            one(2 * i)
            one(2 * i + 1)
            return carry

        lax.fori_loop(0, LH // 2, body, 0)

    def x_copy(d, n):
        return pltpu.make_async_remote_copy(
            src_ref=part.at[d, n, 1 - j], dst_ref=crecv.at[d, n],
            send_sem=x_send.at[d, n], recv_sem=x_recv.at[d, n],
            device_id={"head": sib}, device_id_type=MESH,
        )

    def u_copy(d, n):
        return pltpu.make_async_remote_copy(
            src_ref=part.at[d, n, j], dst_ref=urecv.at[d, n],
            send_sem=z_send.at[d, n], recv_sem=u_recv.at[d, n],
            device_id={"head": h + 2}, device_id_type=MESH,
        )

    def d_copy(d, n):
        return pltpu.make_async_remote_copy(
            src_ref=part.at[d, n, j], dst_ref=drecv.at[d, n],
            send_sem=z_send.at[d, n], recv_sem=d_recv.at[d, n],
            device_id={"head": h - 2}, device_id_type=MESH,
        )

    f32 = jnp.float32

    def process(d, n):
        x_copy(d, n).wait_recv()

        @pl.when(d > z)
        def _():
            @pl.when(z > 0)
            def _():
                u_copy(d, n).wait_recv()
                part[d, n, j] = (
                    part[d, n, j].astype(f32) + crecv[d, n].astype(f32) + urecv[d, n].astype(f32)
                ).astype(jnp.bfloat16)

            @pl.when(z == 0)
            def _():
                part[d, n, j] = (part[d, n, j].astype(f32) + crecv[d, n].astype(f32)).astype(jnp.bfloat16)

            u_copy(d, n).start()

        @pl.when(d < z)
        def _():
            @pl.when(z < Z - 1)
            def _():
                d_copy(d, n).wait_recv()
                part[d, n, j] = (
                    part[d, n, j].astype(f32) + crecv[d, n].astype(f32) + drecv[d, n].astype(f32)
                ).astype(jnp.bfloat16)

            @pl.when(z == Z - 1)
            def _():
                part[d, n, j] = (part[d, n, j].astype(f32) + crecv[d, n].astype(f32)).astype(jnp.bfloat16)

            d_copy(d, n).start()

    low = z < Z // 2
    zm = jnp.where(low, z, Z - 1 - z)

    def dest_of(t):
        paired = jnp.where(t % 2 == 0, Z - 1 - t // 2, t // 2)
        d = jnp.where(t < 2 * zm, paired, Z - 1 - (t - zm))
        return jnp.where(low, d, Z - 1 - d)

    at_end = jnp.logical_or(z == 0, z == Z - 1)

    def project(t, d, first):
        prev = dest_of(jnp.maximum(t - 1, 0))

        def step(n, carry):
            if first:
                w_copy(n).wait()
            y = jnp.dot(att[...], w_ref[n], preferred_element_type=f32).astype(jnp.bfloat16)
            part[d, n, 0] = y[: STEPS * RS]
            part[d, n, 1] = y[STEPS * RS:]
            x_copy(d, n).start()

            @pl.when(jnp.logical_and(at_end, jnp.logical_and(n > 0, d != z)))
            def _():
                process(d, n - 1)

            if not first:
                @pl.when(jnp.logical_not(at_end))
                def _():
                    process(prev, n)
            return carry

        lax.fori_loop(0, NC, step, 0)

        @pl.when(jnp.logical_and(at_end, d != z))
        def _():
            process(d, NC - 1)

    early = [
        pltpu.make_async_copy(bufs[0], bufs[1].at[pl.ds(0, C * SB)], early_sem.at[t])
        for t, bufs in enumerate((kbufs, vbufs))
    ]
    q_copy.wait()
    d_first = dest_of(jnp.int32(0))
    for s in range(STEPS):
        for p in range(1, C):
            origin = lax.rem(c + C - p, C)
            for t in range(2):
                kv_arrival(s, t, origin, j, kv_recv).wait()
                fw_copy(s, t, p).start()
        for step_of, cp in own_copies:
            if step_of == s:
                cp.wait()
        for p in range(1, C):
            origin = lax.rem(c + C - p, C)
            for t in range(2):
                kv_arrival(s, t, origin, 1 - j, fw_recv).wait()
        if s == 0:
            for cp in early:
                cp.start()
        else:
            for cp in early:
                cp.wait()
        attend(d_first, s)
    project(jnp.int32(0), d_first, True)

    def rest(t, carry):
        d = dest_of(t)
        for s in range(STEPS):
            attend(d, s)
        project(t, d, False)
        return carry

    lax.fori_loop(1, Z, rest, 0)

    def o_copy(n, s):
        return pltpu.make_async_copy(
            obuf.at[n, pl.ds(s * RS, RS)],
            out_hbm.at[s, :, pl.ds(pl.multiple_of(n * NW, NW), NW)],
            o_sem.at[n, s],
        )

    def finish(n, carry):
        x_copy(z, n).wait_recv()

        @pl.when(z == 0)
        def _():
            d_copy(z, n).wait_recv()
            obuf[n] = (
                part[z, n, j].astype(f32) + crecv[z, n].astype(f32) + drecv[z, n].astype(f32)
            ).astype(jnp.bfloat16)

        @pl.when(z == Z - 1)
        def _():
            u_copy(z, n).wait_recv()
            obuf[n] = (
                part[z, n, j].astype(f32) + crecv[z, n].astype(f32) + urecv[z, n].astype(f32)
            ).astype(jnp.bfloat16)

        @pl.when(jnp.logical_not(at_end))
        def _():
            d_copy(z, n).wait_recv()
            u_copy(z, n).wait_recv()
            obuf[n] = (
                part[z, n, j].astype(f32) + crecv[z, n].astype(f32)
                + drecv[z, n].astype(f32) + urecv[z, n].astype(f32)
            ).astype(jnp.bfloat16)

        for s in range(STEPS):
            o_copy(n, s).start()
        return carry

    lax.fori_loop(0, NC, finish, 0)

    for s in range(STEPS):
        for p in range(1, C):
            for t in range(2):
                kv_copy(s, t, p).wait_send()
                fw_copy(s, t, p).wait_send()

    def drain(i, carry):
        d = i // NC
        n = i % NC
        x_copy(d, n).wait_send()

        @pl.when(d > z)
        def _():
            u_copy(d, n).wait_send()

        @pl.when(d < z)
        def _():
            d_copy(d, n).wait_send()

        return carry

    lax.fori_loop(0, Z * NC, drain, 0)

    def drain_out(n, carry):
        for s in range(STEPS):
            o_copy(n, s).wait()
        return carry

    lax.fori_loop(0, NC, drain_out, 0)


def solution(mesh):
    C = mesh.shape["ctx"]
    H = mesh.shape["head"]
    Z = H // 2

    def local(queries, key_rows, value_rows, out_weight, span_owner, vertical_blocks, slash_offsets):
        steps, span_rows, width = queries.shape
        depth, DW = out_weight.shape
        LH = width // HD
        RS = span_rows // H
        SB = span_rows // BLK
        NC = DW // NW
        NV, NS = vertical_blocks.shape[1], slash_offsets.shape[1]
        NT = 1 + NV + NS
        bf = jnp.bfloat16
        kv0 = pltpu.VMEM((C * SB, BLK, HD), bf)
        kv1 = pltpu.VMEM((STEPS * C * SB, BLK, HD), bf)
        dma = pltpu.SemaphoreType.DMA
        smem = pl.BlockSpec(memory_space=pltpu.SMEM)
        anyspec = pl.BlockSpec(memory_space=pl.ANY)
        MR = STEPS * RS
        return pl.pallas_call(
            functools.partial(kernel, C, H, LH, RS, NV, NS),
            out_shape=jax.ShapeDtypeStruct((STEPS, RS, DW), bf),
            in_specs=[smem] * 3 + [anyspec] * 4,
            out_specs=anyspec,
            scratch_shapes=[
                pltpu.VMEM((STEPS, span_rows, width), bf),
                kv0, kv1, kv0, kv1,
                pltpu.VMEM((NC, depth, NW), bf),
                pltpu.VMEM((2 * MR, width), bf),
                pltpu.VMEM((Z, NC, 2, MR, NW), bf),
                pltpu.VMEM((Z, NC, MR, NW), bf),
                pltpu.VMEM((Z, NC, MR, NW), bf),
                pltpu.VMEM((Z, NC, MR, NW), bf),
                pltpu.VMEM((NC, MR, NW), bf),
                pltpu.SMEM((STEPS, SB * LH, NT), jnp.int32),
                pltpu.SMEM((STEPS, SB * LH, NT), jnp.float32),
                dma, dma((NC,)), dma((STEPS, 2, SB)),
                dma((STEPS, 2, C)), dma((STEPS, 2, C)), dma((STEPS, 2, C)), dma((STEPS, 2, C)),
                dma((Z, NC)), dma((Z, NC)), dma((Z, NC)), dma((Z, NC)), dma((Z, NC)),
                dma((NC, STEPS)), dma((2,)),
            ],
            compiler_params=pltpu.CompilerParams(
                collective_id=0, has_side_effects=True, vmem_limit_bytes=58 * 1024 * 1024
            ),
            cost_estimate=pl.CostEstimate(
                flops=2 * STEPS * span_rows * depth * DW, bytes_accessed=depth * DW * 2, transcendentals=0
            ),
        )(span_owner, vertical_blocks, slash_offsets, queries, key_rows, value_rows, out_weight)

    in_specs = (
        P(None, "ctx", "head"),
        P(None, "ctx", None),
        P(None, "ctx", None),
        P("head", None),
        P(),
        P(),
        P(),
    )
    return jax.shard_map(
        local, mesh=mesh, in_specs=in_specs, out_specs=P(None, ("ctx", "head"), None), check_vma=False
    )
```

time: 220 us -> 99 us (0.45); the launches traced: 216 us -> 98.6 us
  waiting for transfers between devices: 108 us -> 0 us
  Pallas kernels: 0 us -> 93.6 us
  matrix products: 39.8 us -> 0 us
  local copies, waits for them, and re-layouts: 39.5 us -> 5.01 us
  between operations: 15 us -> 0.01 us
  other arithmetic: 13.9 us -> 0 us
    pallas_call x0 -> x1, Pallas kernels: none -> 93.6 us  [local(): pl.pallas_call(functools.partial(kernel, C, H, LH, RS, NV, NS), out_shape...]
    reduce_scatter x1 -> x0, waiting for transfers between devices: 88.1 us -> none  [local(): lax.psum_scatter(jnp.dot(arranged, out_weight, preferred_element_type=jnp...]
    dot_general x5 -> x0, matrix products: 39.8 us -> none  [the longest x2 17.9 us: attend_tiles(): jnp.einsum('zcs,zvs->zcv', query_tile_set, key_tile_set, preferred_elemen...]
    gather x4 -> x0, local copies, waits for them, and re-layouts: 30.3 us -> none  [the longest x2 15.2 us: attend_tiles(): jnp.take(key_store, stored.reshape(-1), axis=0)]
    all_gather x1 -> x0, waiting for transfers between devices: 19.8 us -> none  [local(): gathered = lax.all_gather(paired, 'ctx', axis=2, tiled=True)]
    select_n x4 -> x0, other arithmetic: 8.97 us -> none  [the longest x2 8.79 us: attend_tiles(): jnp.take(key_store, stored.reshape(-1), axis=0)]
    reduce_sum x4 -> x0, other arithmetic: 3.45 us -> none  [the longest x2 2.53 us: attend_tiles(): totals = jnp.sum(weights, axis=2, keepdims=True)]
    unnamed x13 -> x3, local copies, waits for them, and re-layouts: 1.66 us -> 5.01 us
  transfers between devices with their start and end apart: 2 -> 0, of which waited for: 2 -> 0; matrix products, arithmetic and copies ran while one was open for 3% -> 0% of each run, Pallas kernels for 0% -> 0%
where the time goes in v1:
time: 99 us; the launch traced here: 98.6 us
  Pallas kernels  93.6 us (95%)
  local copies, waits for them, and re-layouts  5.01 us (5%)
    pallas_call x1, Pallas kernels, local(): pl.pallas_call(functools.partial(kernel, C, H, LH, RS, NV, NS), out_shape...  93.6 us
    unnamed x3, local copies, waits for them, and re-layouts  5.01 us

profile of v1, /device:TPU:17, one launch (start us, length us, event | category | flops | bytes accessed | tf_op | source)
XLA Modules:
  0.0 98.6 jit_solution(3428830998882820118)
XLA Ops:
  0.0 1.4 %copy.8.vert = s32[64,4]{1,0:T(8,128)} copy(s32[64,4]{0,1:T(4,128)} %param.12) | data formatting | bytes 2048 | tf_op args[5]
  1.4 1.4 %copy.9.slant = s32[64,4]{1,0:T(8,128)} copy(s32[64,4]{0,1:T(4,128)} %param.13) | data formatting | bytes 2048 | tf_op args[6]
  2.8 93.6 %shard_map.73 = bf16[2,32,8192]{2,1,0:T(8,128)(2,1)} custom-call(s32[2,4]{1,0:T(2,128)} %owner.1, s32[64,4]{1,0:T(8,128)} %copy.8.vert, s32[64,4]{1,0:T(8,128)} %copy.9.slant, bf16[2,256,1024]{2,1,0:T(8,128)(2,1)} %q_hbm.1, bf16[2,256,512]{2,1,0:T(8,128)(2,1)} %k_hbm.1, bf16[2,256,512]{2,1,0:T(8,128)(2,1)} %v_hbm.1, bf16[1024,8192]{1,0:T(8,128)(2,1)} %w_hbm.1), custom_call_target="tpu_custom_call" | custom-call | flops 8589934592 | bytes 16777216 | tf_op jit(solution)/shard_map/pallas_call | solution.py:417
  96.4 2.3 %copy.11 = bf16[2,32,8192]{2,1,0:T(8,128)(2,1)} copy(bf16[2,32,8192]{2,1,0:T(8,128)(2,1)} %shard_map.73) | data formatting | bytes 2097152

commit v2 on v1

--- a/solution.py
+++ b/solution.py
@@ -57,6 +57,9 @@
             w_hbm.at[:, pl.ds(pl.multiple_of(n * NW, NW), NW)], w_ref.at[n], w_sem.at[n]
         )
 
+    for n in range(NC):
+        w_copy(n).start()
+
     barrier = pltpu.get_barrier_semaphore()
     pl.semaphore_signal(barrier, inc=1, device_id={"head": sib}, device_id_type=MESH)
 
@@ -105,19 +108,26 @@
         for p in range(1, C):
             for t in range(2):
                 kv_copy(s, t, p).start()
-    for n in range(NC):
-        w_copy(n).start()
-
-    for s in range(STEPS):
+    low = z < Z // 2
+    zm = jnp.where(low, z, Z - 1 - z)
+
+    def dest_of(t):
+        paired = jnp.where(t % 2 == 0, Z - 1 - t // 2, t // 2)
+        d = jnp.where(t < 2 * zm, paired, Z - 1 - (t - zm))
+        return jnp.where(low, d, Z - 1 - d)
+
+    d_first = dest_of(jnp.int32(0))
+    b_first = (d_first * QR) // BLK
+
+    def fill(s, b):
         place = jnp.int32(0)
         for p in range(C):
             place = jnp.where(owner[s, p] == c, p, place)
-
-        def fill(i, carry, s=s, place=place):
-            b = i // LH
-            lh = i % LH
+        block = (s * C + place) * SB + b
+
+        def one_head(lh, carry):
+            i = b * LH + lh
             head = h * LH + lh
-            block = (s * C + place) * SB + b
 
             def put(tile, chosen, allowed):
                 chosen = jnp.where(allowed, chosen, block)
@@ -127,19 +137,22 @@
                 tab_idx[s, i, tile] = (step * C + holder) * SB + chosen - span * SB
                 tab_bias[s, i, tile] = jnp.where(allowed, 0.0, -1e30).astype(jnp.float32)
 
-            vs = [vert[head, a] for a in range(NV)]
+            vs = [vert[a, head] for a in range(NV)]
             put(0, block, block == block)
             for a in range(NV):
                 put(1 + a, vs[a], vs[a] < block)
             for a in range(NS):
-                row = block - slant[head, a]
+                row = block - slant[a, head]
                 ok = row >= 0
                 for x in vs:
                     ok = jnp.logical_and(ok, row != x)
                 put(1 + NV + a, row, ok)
             return carry
 
-        lax.fori_loop(0, SB * LH, fill, 0)
+        lax.fori_loop(0, LH, one_head, 0)
+
+    for s in range(STEPS):
+        fill(s, b_first)
 
     scale = math.log2(math.e) / math.sqrt(HD)
 
@@ -183,8 +196,7 @@
             vt = jnp.concatenate([tile(vbufs, t) for t in range(NT)], axis=0)
             mixed = jnp.dot(wt, vt, preferred_element_type=jnp.float32) / tot
             mixed = mixed.astype(jnp.bfloat16)
-            att[pl.ds(s * RS, RS), hc] = mixed[:RS]
-            att[pl.ds((STEPS + s) * RS, RS), hc] = mixed[RS:]
+            att[pl.ds(s * QR, QR), hc] = mixed
 
         def body(i, carry):
             one(2 * i)
@@ -193,105 +205,122 @@
 
         lax.fori_loop(0, LH // 2, body, 0)
 
-    def x_copy(d, n):
+    def x_copy(d, n, s):
         return pltpu.make_async_remote_copy(
-            src_ref=part.at[d, n, 1 - j], dst_ref=crecv.at[d, n],
-            send_sem=x_send.at[d, n], recv_sem=x_recv.at[d, n],
+            src_ref=part.at[d, n, s, 1 - j], dst_ref=crecv.at[d, n, s],
+            send_sem=x_send.at[d, n, s], recv_sem=x_recv.at[d, n, s],
             device_id={"head": sib}, device_id_type=MESH,
         )
 
-    def u_copy(d, n):
+    def u_copy(d, n, s):
         return pltpu.make_async_remote_copy(
-            src_ref=part.at[d, n, j], dst_ref=urecv.at[d, n],
-            send_sem=z_send.at[d, n], recv_sem=u_recv.at[d, n],
+            src_ref=part.at[d, n, s, j], dst_ref=urecv.at[d, n, s],
+            send_sem=z_send.at[d, n, s], recv_sem=u_recv.at[d, n, s],
             device_id={"head": h + 2}, device_id_type=MESH,
         )
 
-    def d_copy(d, n):
+    def d_copy(d, n, s):
         return pltpu.make_async_remote_copy(
-            src_ref=part.at[d, n, j], dst_ref=drecv.at[d, n],
-            send_sem=z_send.at[d, n], recv_sem=d_recv.at[d, n],
+            src_ref=part.at[d, n, s, j], dst_ref=drecv.at[d, n, s],
+            send_sem=z_send.at[d, n, s], recv_sem=d_recv.at[d, n, s],
             device_id={"head": h - 2}, device_id_type=MESH,
         )
 
     f32 = jnp.float32
 
-    def process(d, n):
-        x_copy(d, n).wait_recv()
+    def process(d, n, s):
+        x_copy(d, n, s).wait_recv()
+
+        def ready(*more):
+            total = part[d, n, s, j].astype(f32) + crecv[d, n, s].astype(f32)
+            for buf in more:
+                total = total + buf[d, n, s].astype(f32)
+            part[d, n, s, j] = total.astype(jnp.bfloat16)
 
         @pl.when(d > z)
         def _():
             @pl.when(z > 0)
             def _():
-                u_copy(d, n).wait_recv()
-                part[d, n, j] = (
-                    part[d, n, j].astype(f32) + crecv[d, n].astype(f32) + urecv[d, n].astype(f32)
-                ).astype(jnp.bfloat16)
+                u_copy(d, n, s).wait_recv()
+                ready(urecv)
 
             @pl.when(z == 0)
             def _():
-                part[d, n, j] = (part[d, n, j].astype(f32) + crecv[d, n].astype(f32)).astype(jnp.bfloat16)
-
-            u_copy(d, n).start()
+                ready()
+
+            u_copy(d, n, s).start()
 
         @pl.when(d < z)
         def _():
             @pl.when(z < Z - 1)
             def _():
-                d_copy(d, n).wait_recv()
-                part[d, n, j] = (
-                    part[d, n, j].astype(f32) + crecv[d, n].astype(f32) + drecv[d, n].astype(f32)
-                ).astype(jnp.bfloat16)
+                d_copy(d, n, s).wait_recv()
+                ready(drecv)
 
             @pl.when(z == Z - 1)
             def _():
-                part[d, n, j] = (part[d, n, j].astype(f32) + crecv[d, n].astype(f32)).astype(jnp.bfloat16)
-
-            d_copy(d, n).start()
-
-    low = z < Z // 2
-    zm = jnp.where(low, z, Z - 1 - z)
-
-    def dest_of(t):
-        paired = jnp.where(t % 2 == 0, Z - 1 - t // 2, t // 2)
-        d = jnp.where(t < 2 * zm, paired, Z - 1 - (t - zm))
-        return jnp.where(low, d, Z - 1 - d)
+                ready()
+
+            d_copy(d, n, s).start()
 
     at_end = jnp.logical_or(z == 0, z == Z - 1)
 
-    def project(t, d, first):
-        prev = dest_of(jnp.maximum(t - 1, 0))
-
+    def send_parts(d, n, y, ss):
+        for i, s in enumerate(ss):
+            for jj in range(2):
+                part[d, n, s, jj] = y[(2 * i + jj) * RS:(2 * i + jj + 1) * RS]
+            x_copy(d, n, s).start()
+
+    def project_first(d, s):
         def step(n, carry):
-            if first:
+            if s == 0:
                 w_copy(n).wait()
-            y = jnp.dot(att[...], w_ref[n], preferred_element_type=f32).astype(jnp.bfloat16)
-            part[d, n, 0] = y[: STEPS * RS]
-            part[d, n, 1] = y[STEPS * RS:]
-            x_copy(d, n).start()
+            y = jnp.dot(att[pl.ds(s * QR, QR)], w_ref[n], preferred_element_type=f32)
+            send_parts(d, n, y.astype(jnp.bfloat16), (s,))
+
+            @pl.when(jnp.logical_and(at_end, n > 0))
+            def _():
+                process(d, n - 1, s)
+
+            return carry
+
+        lax.fori_loop(0, NC, step, 0)
+
+        @pl.when(at_end)
+        def _():
+            process(d, NC - 1, s)
+
+    def project(t, d):
+        prev = dest_of(t - 1)
+
+        def step(n, carry):
+            y = jnp.dot(att[...], w_ref[n], preferred_element_type=f32)
+            send_parts(d, n, y.astype(jnp.bfloat16), range(STEPS))
 
             @pl.when(jnp.logical_and(at_end, jnp.logical_and(n > 0, d != z)))
             def _():
-                process(d, n - 1)
-
-            if not first:
-                @pl.when(jnp.logical_not(at_end))
-                def _():
-                    process(prev, n)
+                for s in range(STEPS):
+                    process(d, n - 1, s)
+
+            @pl.when(jnp.logical_not(at_end))
+            def _():
+                for s in range(STEPS):
+                    process(prev, n, s)
+
             return carry
 
         lax.fori_loop(0, NC, step, 0)
 
         @pl.when(jnp.logical_and(at_end, d != z))
         def _():
-            process(d, NC - 1)
+            for s in range(STEPS):
+                process(d, NC - 1, s)
 
     early = [
         pltpu.make_async_copy(bufs[0], bufs[1].at[pl.ds(0, C * SB)], early_sem.at[t])
         for t, bufs in enumerate((kbufs, vbufs))
     ]
     q_copy.wait()
-    d_first = dest_of(jnp.int32(0))
     for s in range(STEPS):
         for p in range(1, C):
             origin = lax.rem(c + C - p, C)
@@ -312,78 +341,93 @@
             for cp in early:
                 cp.wait()
         attend(d_first, s)
-    project(jnp.int32(0), d_first, True)
+        project_first(d_first, s)
+    for k in range(1, SB):
+        for s in range(STEPS):
+            fill(s, lax.rem(b_first + k, SB))
 
     def rest(t, carry):
         d = dest_of(t)
         for s in range(STEPS):
             attend(d, s)
-        project(t, d, False)
+        project(t, d)
         return carry
 
     lax.fori_loop(1, Z, rest, 0)
 
     def o_copy(n, s):
         return pltpu.make_async_copy(
-            obuf.at[n, pl.ds(s * RS, RS)],
+            obuf.at[n, s],
             out_hbm.at[s, :, pl.ds(pl.multiple_of(n * NW, NW), NW)],
             o_sem.at[n, s],
         )
 
     def finish(n, carry):
-        x_copy(z, n).wait_recv()
-
-        @pl.when(z == 0)
-        def _():
-            d_copy(z, n).wait_recv()
-            obuf[n] = (
-                part[z, n, j].astype(f32) + crecv[z, n].astype(f32) + drecv[z, n].astype(f32)
-            ).astype(jnp.bfloat16)
-
-        @pl.when(z == Z - 1)
-        def _():
-            u_copy(z, n).wait_recv()
-            obuf[n] = (
-                part[z, n, j].astype(f32) + crecv[z, n].astype(f32) + urecv[z, n].astype(f32)
-            ).astype(jnp.bfloat16)
-
-        @pl.when(jnp.logical_not(at_end))
-        def _():
-            d_copy(z, n).wait_recv()
-            u_copy(z, n).wait_recv()
-            obuf[n] = (
-                part[z, n, j].astype(f32) + crecv[z, n].astype(f32)
-                + drecv[z, n].astype(f32) + urecv[z, n].astype(f32)
-            ).astype(jnp.bfloat16)
-
         for s in range(STEPS):
+            def done(*more, s=s):
+                total = part[z, n, s, j].astype(f32) + crecv[z, n, s].astype(f32)
+                for buf in more:
+                    total = total + buf[z, n, s].astype(f32)
+                obuf[n, s] = total.astype(jnp.bfloat16)
+
+            x_copy(z, n, s).wait_recv()
+
+            @pl.when(z == 0)
+            def _():
+                d_copy(z, n, s).wait_recv()
+                done(drecv)
+
+            @pl.when(z == Z - 1)
+            def _():
+                u_copy(z, n, s).wait_recv()
+                done(urecv)
+
+            @pl.when(jnp.logical_not(at_end))
+            def _():
+                d_copy(z, n, s).wait_recv()
+                u_copy(z, n, s).wait_recv()
+                done(drecv, urecv)
+
             o_copy(n, s).start()
         return carry
 
-    lax.fori_loop(0, NC, finish, 0)
+    def drain_z(i, carry):
+        d = i // NC
+        n = i % NC
+
+        @pl.when(d > z)
+        def _():
+            for s in range(STEPS):
+                u_copy(d, n, s).wait_send()
+
+        @pl.when(d < z)
+        def _():
+            for s in range(STEPS):
+                d_copy(d, n, s).wait_send()
+
+        return carry
+
+    def drain_x(i, carry):
+        for s in range(STEPS):
+            x_copy(i // NC, i % NC, s).wait_send()
+        return carry
 
     for s in range(STEPS):
         for p in range(1, C):
             for t in range(2):
                 kv_copy(s, t, p).wait_send()
                 fw_copy(s, t, p).wait_send()
-
-    def drain(i, carry):
-        d = i // NC
-        n = i % NC
-        x_copy(d, n).wait_send()
-
-        @pl.when(d > z)
-        def _():
-            u_copy(d, n).wait_send()
-
-        @pl.when(d < z)
-        def _():
-            d_copy(d, n).wait_send()
-
-        return carry
-
-    lax.fori_loop(0, Z * NC, drain, 0)
+    lax.fori_loop(0, Z * NC, drain_x, 0)
+
+    @pl.when(jnp.logical_not(at_end))
+    def _():
+        lax.fori_loop(0, Z * NC, drain_z, 0)
+
+    lax.fori_loop(0, NC, finish, 0)
+
+    @pl.when(at_end)
+    def _():
+        lax.fori_loop(0, Z * NC, drain_z, 0)
 
     def drain_out(n, carry):
         for s in range(STEPS):
@@ -424,16 +468,16 @@
                 kv0, kv1, kv0, kv1,
                 pltpu.VMEM((NC, depth, NW), bf),
                 pltpu.VMEM((2 * MR, width), bf),
-                pltpu.VMEM((Z, NC, 2, MR, NW), bf),
-                pltpu.VMEM((Z, NC, MR, NW), bf),
-                pltpu.VMEM((Z, NC, MR, NW), bf),
-                pltpu.VMEM((Z, NC, MR, NW), bf),
-                pltpu.VMEM((NC, MR, NW), bf),
+                pltpu.VMEM((Z, NC, STEPS, 2, RS, NW), bf),
+                pltpu.VMEM((Z, NC, STEPS, RS, NW), bf),
+                pltpu.VMEM((Z, NC, STEPS, RS, NW), bf),
+                pltpu.VMEM((Z, NC, STEPS, RS, NW), bf),
+                pltpu.VMEM((NC, STEPS, RS, NW), bf),
                 pltpu.SMEM((STEPS, SB * LH, NT), jnp.int32),
                 pltpu.SMEM((STEPS, SB * LH, NT), jnp.float32),
                 dma, dma((NC,)), dma((STEPS, 2, SB)),
                 dma((STEPS, 2, C)), dma((STEPS, 2, C)), dma((STEPS, 2, C)), dma((STEPS, 2, C)),
-                dma((Z, NC)), dma((Z, NC)), dma((Z, NC)), dma((Z, NC)), dma((Z, NC)),
+                *[dma((Z, NC, STEPS))] * 5,
                 dma((NC, STEPS)), dma((2,)),
             ],
             compiler_params=pltpu.CompilerParams(
@@ -442,7 +486,7 @@
             cost_estimate=pl.CostEstimate(
                 flops=2 * STEPS * span_rows * depth * DW, bytes_accessed=depth * DW * 2, transcendentals=0
             ),
-        )(span_owner, vertical_blocks, slash_offsets, queries, key_rows, value_rows, out_weight)
+        )(span_owner, vertical_blocks.T, slash_offsets.T, queries, key_rows, value_rows, out_weight)
 
     in_specs = (
         P(None, "ctx", "head"),

time: 99 us -> 97.2 us (0.982)
  local copies, waits for them, and re-layouts: 5.01 us -> 2.26 us
    unnamed x3 -> x1, local copies, waits for them, and re-layouts: 5.01 us -> 2.26 us
where the time goes in v2:
time: 97.2 us; the launch traced here: 96.7 us
  Pallas kernels  94.5 us (97%)
  local copies, waits for them, and re-layouts  2.26 us (2%)
    pallas_call x1, Pallas kernels, local(): pl.pallas_call(functools.partial(kernel, C, H, LH, RS, NV, NS), out_shape...  94.5 us
    unnamed x1, local copies, waits for them, and re-layouts  2.26 us

profile of v2, /device:TPU:17, one launch (start us, length us, event | category | flops | bytes accessed | tf_op | source)
XLA Modules:
  0.0 96.7 jit_solution(17577934939850715547)
XLA Ops:
  0.0 94.5 %shard_map.73 = bf16[2,32,8192]{2,1,0:T(8,128)(2,1)} custom-call(s32[2,4]{1,0:T(2,128)} %owner.1, s32[4,64]{1,0:T(4,128)} %bitcast.2, s32[4,64]{1,0:T(4,128)} %bitcast.3, bf16[2,256,1024]{2,1,0:T(8,128)(2,1)} %q_hbm.1, bf16[2,256,512]{2,1,0:T(8,128)(2,1)} %k_hbm.1, bf16[2,256,512]{2,1,0:T(8,128)(2,1)} %v_hbm.1, bf16[1024,8192]{1,0:T(8,128)(2,1)} %w_hbm.1), custom_call_target="tpu_custom_call" | custom-call | flops 8589934592 | bytes 16777216 | tf_op jit(solution)/shard_map/pallas_call | solution.py:461
  94.5 2.3 %copy.9 = bf16[2,32,8192]{2,1,0:T(8,128)(2,1)} copy(bf16[2,32,8192]{2,1,0:T(8,128)(2,1)} %shard_map.73) | data formatting | bytes 2097152

commit v3 on v2

--- a/solution.py
+++ b/solution.py
@@ -20,7 +20,7 @@
 def kernel(
     C, H, LH, RS, NV, NS,
     owner, vert, slant, q_hbm, k_hbm, v_hbm, w_hbm, out_hbm,
-    q_ref, k0, k1, v0, v1, w_ref, att, part, crecv, urecv, drecv, obuf, tab_idx, tab_bias,
+    q_ref, k0, k1, v0, v1, kt_ref, w_ref, att, part, crecv, urecv, drecv, obuf, tab_idx, tab_bias,
     load_sem, w_sem, own_sem, kv_send, kv_recv, fw_send, fw_recv,
     x_send, x_recv, z_send, u_recv, d_recv, o_sem, early_sem,
 ):
@@ -40,12 +40,15 @@
     cols = pl.ds(pl.multiple_of(kv_head * HD, HD), HD)
     own_rows = pl.ds(pl.multiple_of(j * BLK, BLK), BLK)
 
+    def base(s, t):
+        return s * C * SB if t == 1 else 0
+
     own_copies = []
     for s in range(STEPS):
         for t, (src, bufs) in enumerate(((k_hbm, kbufs), (v_hbm, vbufs))):
             for b in range(SB):
                 cp = pltpu.make_async_copy(
-                    src.at[s, pl.ds(b * BLK, BLK), cols], bufs[s].at[s * C * SB + SB * c + b], own_sem.at[s, t, b]
+                    src.at[s, pl.ds(b * BLK, BLK), cols], bufs[s].at[base(s, t) + SB * c + b], own_sem.at[s, t, b]
                 )
                 cp.start()
                 own_copies.append((s, cp))
@@ -80,7 +83,7 @@
         buf = (kbufs, vbufs)[t][s]
         return pltpu.make_async_remote_copy(
             src_ref=src.at[s, own_rows, cols],
-            dst_ref=buf.at[s * C * SB + SB * c + j],
+            dst_ref=buf.at[base(s, t) + SB * c + j],
             send_sem=kv_send.at[s, t, p],
             recv_sem=kv_recv.at[s, t, c],
             device_id={"ctx": lax.rem(c + p, C)},
@@ -89,15 +92,15 @@
 
     def kv_arrival(s, t, origin, block, sem):
         buf = (kbufs, vbufs)[t][s]
-        dst = buf.at[s * C * SB + SB * origin + block]
+        dst = buf.at[base(s, t) + SB * origin + block]
         return pltpu.make_async_copy(dst, dst, sem.at[s, t, origin])
 
     def fw_copy(s, t, p):
         origin = lax.rem(c + C - p, C)
         buf = (kbufs, vbufs)[t][s]
         return pltpu.make_async_remote_copy(
-            src_ref=buf.at[s * C * SB + SB * origin + j],
-            dst_ref=buf.at[s * C * SB + SB * origin + j],
+            src_ref=buf.at[base(s, t) + SB * origin + j],
+            dst_ref=buf.at[base(s, t) + SB * origin + j],
             send_sem=fw_send.at[s, t, p],
             recv_sem=fw_recv.at[s, t, origin],
             device_id={"head": sib},
@@ -156,30 +159,25 @@
 
     scale = math.log2(math.e) / math.sqrt(HD)
 
-    def attend(d, s):
-        r0 = pl.multiple_of(d * QR, QR)
-        b = r0 // BLK
-        within = r0 - b * BLK
-        row_ids = lax.broadcasted_iota(jnp.int32, (QR, BLK), 0) + within
-        col_ids = lax.broadcasted_iota(jnp.int32, (QR, BLK), 1)
-        causal = col_ids <= row_ids
+    row_ids = lax.broadcasted_iota(jnp.int32, (BLK, BLK), 0)
+    col_ids = lax.broadcasted_iota(jnp.int32, (BLK, BLK), 1)
+
+    def attend(b, s):
+        rows = pl.ds(pl.multiple_of(b * BLK, BLK), BLK)
 
         def one(lh):
             hc = pl.ds(pl.multiple_of(lh * HD, HD), HD)
             i = b * LH + lh
-            qt = q_ref[s, pl.ds(r0, QR), hc]
+            qt = q_ref[s, rows, hc]
             ids = [tab_idx[s, i, t] for t in range(NT)]
 
-            def tile(bufs, t):
-                return bufs[s][ids[t]]
-
-            kt = jnp.concatenate([tile(kbufs, t) for t in range(NT)], axis=0)
-            sc = lax.dot_general(qt, kt, (((1,), (1,)), ((), ())), preferred_element_type=jnp.float32)
+            kt = jnp.concatenate([kt_ref[ids[t]] for t in range(NT)], axis=1)
+            sc = jnp.dot(qt, kt, preferred_element_type=jnp.float32)
             pieces = []
             for t in range(NT):
                 x = sc[:, t * BLK:(t + 1) * BLK] * scale
                 if t == 0:
-                    x = jnp.where(causal, x, -1e30)
+                    x = jnp.where(col_ids <= row_ids, x, -1e30)
                 else:
                     x = x + tab_bias[s, i, t]
                 pieces.append(x)
@@ -193,10 +191,9 @@
                 tot = tot + x
             tot = jnp.sum(tot, axis=1, keepdims=True)
             wt = jnp.concatenate([x.astype(jnp.bfloat16) for x in ws], axis=1)
-            vt = jnp.concatenate([tile(vbufs, t) for t in range(NT)], axis=0)
-            mixed = jnp.dot(wt, vt, preferred_element_type=jnp.float32) / tot
-            mixed = mixed.astype(jnp.bfloat16)
-            att[pl.ds(s * QR, QR), hc] = mixed
+            vt = jnp.concatenate([vbufs[s][ids[t]] for t in range(NT)], axis=0)
+            mixed = jnp.dot(wt, vt, preferred_element_type=jnp.float32) * (1.0 / tot)
+            att[s, rows, hc] = mixed.astype(jnp.bfloat16)
 
         def body(i, carry):
             one(2 * i)
@@ -271,11 +268,14 @@
                 part[d, n, s, jj] = y[(2 * i + jj) * RS:(2 * i + jj + 1) * RS]
             x_copy(d, n, s).start()
 
+    def rows_of(d, s):
+        return att[s, pl.ds(pl.multiple_of(d * QR, QR), QR), :]
+
     def project_first(d, s):
         def step(n, carry):
             if s == 0:
                 w_copy(n).wait()
-            y = jnp.dot(att[pl.ds(s * QR, QR)], w_ref[n], preferred_element_type=f32)
+            y = jnp.dot(rows_of(d, s), w_ref[n], preferred_element_type=f32)
             send_parts(d, n, y.astype(jnp.bfloat16), (s,))
 
             @pl.when(jnp.logical_and(at_end, n > 0))
@@ -294,7 +294,8 @@
         prev = dest_of(t - 1)
 
         def step(n, carry):
-            y = jnp.dot(att[...], w_ref[n], preferred_element_type=f32)
+            lhs = jnp.concatenate([rows_of(d, s) for s in range(STEPS)], axis=0)
+            y = jnp.dot(lhs, w_ref[n], preferred_element_type=f32)
             send_parts(d, n, y.astype(jnp.bfloat16), range(STEPS))
 
             @pl.when(jnp.logical_and(at_end, jnp.logical_and(n > 0, d != z)))
@@ -317,8 +318,7 @@
                 process(d, NC - 1, s)
 
     early = [
-        pltpu.make_async_copy(bufs[0], bufs[1].at[pl.ds(0, C * SB)], early_sem.at[t])
-        for t, bufs in enumerate((kbufs, vbufs))
+        pltpu.make_async_copy(v0, v1.at[pl.ds(0, C * SB)], early_sem)
     ]
     q_copy.wait()
     for s in range(STEPS):
@@ -334,13 +334,18 @@
             origin = lax.rem(c + C - p, C)
             for t in range(2):
                 kv_arrival(s, t, origin, 1 - j, fw_recv).wait()
+        def turn(i, carry, s=s):
+            kt_ref[s * C * SB + i] = kbufs[s][i].T
+            return carry
+
+        lax.fori_loop(0, C * SB, turn, 0)
         if s == 0:
             for cp in early:
                 cp.start()
         else:
             for cp in early:
                 cp.wait()
-        attend(d_first, s)
+        attend(b_first, s)
         project_first(d_first, s)
     for k in range(1, SB):
         for s in range(STEPS):
@@ -348,8 +353,17 @@
 
     def rest(t, carry):
         d = dest_of(t)
-        for s in range(STEPS):
-            attend(d, s)
+        b = (d * QR) // BLK
+        fresh = t > 0
+        for before in range(Z):
+            other = (dest_of(jnp.int32(before)) * QR) // BLK
+            fresh = jnp.logical_and(fresh, jnp.logical_or(before >= t, other != b))
+
+        @pl.when(fresh)
+        def _():
+            for s in range(STEPS):
+                attend(b, s)
+
         project(t, d)
         return carry
 
@@ -453,11 +467,11 @@
         NT = 1 + NV + NS
         bf = jnp.bfloat16
         kv0 = pltpu.VMEM((C * SB, BLK, HD), bf)
+        kt = pltpu.VMEM((STEPS * C * SB, HD, BLK), bf)
         kv1 = pltpu.VMEM((STEPS * C * SB, BLK, HD), bf)
         dma = pltpu.SemaphoreType.DMA
         smem = pl.BlockSpec(memory_space=pltpu.SMEM)
         anyspec = pl.BlockSpec(memory_space=pl.ANY)
-        MR = STEPS * RS
         return pl.pallas_call(
             functools.partial(kernel, C, H, LH, RS, NV, NS),
             out_shape=jax.ShapeDtypeStruct((STEPS, RS, DW), bf),
@@ -465,9 +479,9 @@
             out_specs=anyspec,
             scratch_shapes=[
                 pltpu.VMEM((STEPS, span_rows, width), bf),
-                kv0, kv1, kv0, kv1,
+                kv0, kv0, kv0, kv1, kt,
                 pltpu.VMEM((NC, depth, NW), bf),
-                pltpu.VMEM((2 * MR, width), bf),
+                pltpu.VMEM((STEPS, span_rows, width), bf),
                 pltpu.VMEM((Z, NC, STEPS, 2, RS, NW), bf),
                 pltpu.VMEM((Z, NC, STEPS, RS, NW), bf),
                 pltpu.VMEM((Z, NC, STEPS, RS, NW), bf),
@@ -478,7 +492,7 @@
                 dma, dma((NC,)), dma((STEPS, 2, SB)),
                 dma((STEPS, 2, C)), dma((STEPS, 2, C)), dma((STEPS, 2, C)), dma((STEPS, 2, C)),
                 *[dma((Z, NC, STEPS))] * 5,
-                dma((NC, STEPS)), dma((2,)),
+                dma((NC, STEPS)), dma,
             ],
             compiler_params=pltpu.CompilerParams(
                 collective_id=0, has_side_effects=True, vmem_limit_bytes=58 * 1024 * 1024

time: 97.2 us -> 93.5 us (0.962)
  Pallas kernels: 94.5 us -> 91.1 us
    pallas_call x1, Pallas kernels: 94.5 us -> 91.1 us  [local(): pl.pallas_call(functools.partial(kernel, C, H, LH, RS, NV, NS), out_shape...]
where the time goes in v3:
time: 93.5 us; the launch traced here: 93.4 us
  Pallas kernels  91.1 us (97%)
  local copies, waits for them, and re-layouts  2.26 us (2%)
    pallas_call x1, Pallas kernels, local(): pl.pallas_call(functools.partial(kernel, C, H, LH, RS, NV, NS), out_shape...  91.1 us
    unnamed x1, local copies, waits for them, and re-layouts  2.26 us

profile of v3, /device:TPU:17, one launch (start us, length us, event | category | flops | bytes accessed | tf_op | source)
XLA Modules:
  0.0 93.4 jit_solution(614700841056404914)
XLA Ops:
  0.0 91.1 %shard_map.73 = bf16[2,32,8192]{2,1,0:T(8,128)(2,1)} custom-call(s32[2,4]{1,0:T(2,128)} %owner.1, s32[4,64]{1,0:T(4,128)} %bitcast.2, s32[4,64]{1,0:T(4,128)} %bitcast.3, bf16[2,256,1024]{2,1,0:T(8,128)(2,1)} %q_hbm.1, bf16[2,256,512]{2,1,0:T(8,128)(2,1)} %k_hbm.1, bf16[2,256,512]{2,1,0:T(8,128)(2,1)} %v_hbm.1, bf16[1024,8192]{1,0:T(8,128)(2,1)} %w_hbm.1), custom_call_target="tpu_custom_call" | custom-call | flops 8589934592 | bytes 16777216 | tf_op jit(solution)/shard_map/pallas_call | solution.py:475
  91.1 2.3 %copy.9 = bf16[2,32,8192]{2,1,0:T(8,128)(2,1)} copy(bf16[2,32,8192]{2,1,0:T(8,128)(2,1)} %shard_map.73) | data formatting | bytes 2097152
